TPU v7x, 32 devices: a whole 2x2x4 slice. The times are simulated.
32 devices in a mesh: grp: 2 (over y), lon: 4 (over x, core), lat: 4 (over z).
Axes of the slice: x: 2, y: 2, z: 4, core: 2. Of those that a mesh axis runs over, the one named last changes fastest.
Arguments:
- grid_field: bfloat16 [192, 1440, 256], P(('grp', 'lat'), 'lon'), parts along dimension 0, may hold values from -6 to 6
- weights: bfloat16 [512, 2, 256, 256], P(('lon', 'lat')), may hold values from -0.25 to 0.25
Outputs:
- upsampled: bfloat16 [192, 2880, 256], P(('grp', 'lat'), 'lon'), parts along dimension 0
There are 2 independent parts, one for each index of `grp`. A program takes and returns all parts, laid end to end along the dimension named above; an argument that names none is the same for every part. Nothing has to cross between parts.
All inputs are finite; a program needn't handle non-finite values.
Results may differ from a plain program's by a relative error of at most 0.014.
Values may be sent and summed in bfloat16 or wider, within the bound.
A program may use at most 320 MiB of HBM per device.

v0:
```python
import math
import jax
import jax.numpy as jnp
from jax import lax
from jax.sharding import PartitionSpec as P

NLON = 1440
M = 512


def analysis_table(lon_index):
    mode_index = jnp.arange(M, dtype=jnp.int32)
    norm_scale = 1.0 / math.sqrt(NLON)
    phase_index = mode_index[:, None] * lon_index[None, :] % NLON
    angles = 2.0 * math.pi / NLON * phase_index.astype(jnp.float32)
    table = jnp.stack([jnp.cos(angles) * norm_scale, -jnp.sin(angles) * norm_scale], 1)
    return table.reshape(2 * M, lon_index.shape[0]).astype(jnp.bfloat16)


def synthesis_table(out_index):
    mode_index = jnp.arange(M, dtype=jnp.int32)
    norm_scale = 1.0 / math.sqrt(NLON)
    phase_out = mode_index[:, None] * out_index[None, :] % (2 * NLON)
    angles_out = 2.0 * math.pi / (2 * NLON) * phase_out.astype(jnp.float32)
    factor = jnp.where(mode_index == 0, 1.0, 2.0).astype(jnp.float32)[:, None] * norm_scale
    table = jnp.stack([jnp.cos(angles_out) * factor, -jnp.sin(angles_out) * factor], 1)
    return table.reshape(2 * M, out_index.shape[0]).astype(jnp.bfloat16)


def mix_modes(slab_modes, portion):
    re_part = portion[:, 0]
    im_part = portion[:, 1]
    wide_weight = jnp.stack(
        [jnp.concatenate([re_part, im_part], -1), jnp.concatenate([-im_part, re_part], -1)], 1
    )
    return jnp.einsum(
        "mplc,mpcd->mld", slab_modes, wide_weight, preferred_element_type=jnp.float32
    ).astype(jnp.bfloat16)


def on_device(grid_field, weights):
    lat_rows, lon_dev, channels = grid_field.shape
    lon_count = lax.axis_size("lon")
    lon_rank = lax.axis_index("lon")
    modes_dev = M // lon_count
    lon_index = lon_rank * lon_dev + jnp.arange(lon_dev, dtype=jnp.int32)
    fwd_local = analysis_table(lon_index)
    table_rows = fwd_local
    summed = lax.psum_scatter(
        jnp.einsum(
            "kn,lnc->klc", table_rows, grid_field, preferred_element_type=jnp.float32
        ).astype(jnp.bfloat16),
        "lon",
        scatter_dimension=0,
        tiled=True,
    )
    lat_count = lax.axis_size("lat")
    own_modes = modes_dev // lat_count
    moved = lax.all_to_all(
        summed.reshape(lat_count, 2 * own_modes, lat_rows, channels), "lat", 0, 0, tiled=True
    )
    spectrum = (
        moved.reshape(lat_count, own_modes, 2, lat_rows, channels)
        .transpose(1, 2, 0, 3, 4)
        .reshape(own_modes, 2, lat_count * lat_rows, channels)
    )
    mixed_own = mix_modes(spectrum, weights)
    back = mixed_own.reshape(own_modes, lat_count, lat_rows, 2 * channels).transpose(1, 0, 2, 3)
    mixed_spec = lax.all_to_all(back, "lat", 0, 0, tiled=True).reshape(
        modes_dev, lat_rows, 2 * channels
    )
    out_dev = 2 * NLON // lon_count
    out_index = lon_rank * out_dev + jnp.arange(out_dev, dtype=jnp.int32)
    inv_local = synthesis_table(out_index).reshape(M, 2, out_dev)
    portion = lax.all_gather(mixed_spec, "lon", axis=0, tiled=True)
    count = portion.shape[0]
    table_rows = inv_local
    parted = portion.reshape(count, lat_rows, 2, channels)
    running = jnp.einsum("mlpc,mpn->lnc", parted, table_rows, preferred_element_type=jnp.float32)
    return running.astype(jnp.bfloat16)


def solution(mesh):
    placed = (P(("grp", "lat"), "lon", None), P(("lon", "lat"), None, None, None))
    return jax.shard_map(
        on_device,
        mesh=mesh,
        in_specs=placed,
        out_specs=P(("grp", "lat"), "lon", None),
        check_vma=False,
    )
```

profile of v0, /device:TPU:0, one launch (start us, length us, event | category | flops | bytes accessed | tf_op | source)
XLA Modules:
  0.0 409.2 jit_solution(5694878123159895570)
XLA Ops:
  6.5 0.0 reduce-scatter.2.cloned.1.call-start
  6.5 3.6 multiply_convert_fusion.3
  10.1 0.1 pad_maximum_fusion
  10.2 1.2 copy.24
  11.4 0.6 convert_element_type.48
  12.1 11.8 %convolution_convert_fusion = bf16[1024,24,256]{2,0,1:T(8,128)(2,1)} fusion(bf16[24,360,256]{2,1,0:T(8,128)(2,1)} %param.2, bf16[1024,360]{1,0:T(8,128)(2,1)S(1)} %convert_element_type.48), kind=kOutput, calls=%fused_computation.8 | convolution fusion | flops 4536139776 | bytes 17743872 | tf_op jit(solution)/shard_map/kn,lnc->klc/dot_general | solution.py:50
  23.9 0.0 reduce-scatter.2.cloned.1.call-update
  23.9 101.9 %reduce-scatter.2.cloned.1.call-done = bf16[256,24,256]{2,0,1:T(8,128)(2,1)} async-done(((bf16[1024,24,256]{2,0,1:T(8,128)(2,1)}), bf16[256,24,256]{2,0,1:T(8,128)(2,1)}) %reduce-scatter.2.cloned.1.call-update) | async-done | bytes 3145744 | tf_op jit(solution)/shard_map/reduce_scatter | solution.py:49
  125.8 4.0 copy.26
  129.8 4.6 %all-to-all-start = ((bf16[4,64,24,256]{3,1,2,0:T(8,128)(2,1)}), bf16[4,64,24,256]{3,1,2,0:T(8,128)(2,1)S(1)}, u32[]{:S(2)}, u32[]{:S(2)}) async-start(bf16[4,64,24,256]{3,1,2,0:T(8,128)(2,1)} %copy.26), calls=%async_computation.1 | async-start | bytes 6291456 | tf_op jit(solution)/shard_map/all_to_all | solution.py:59
  134.5 0.0 all-gather.2.cloned.1.call-start
  134.5 2.5 fusion.22
  136.9 3.8 slice_bitcast_fusion
  140.8 6.3 %maximum_bitcast_fusion = (bf16[32,1,256,512]{3,2,1,0:T(8,128)(2,1)}, bf16[32,1,256,512]{3,2,1,0:T(8,128)(2,1)}) fusion(bf16[32,256,256]{2,1,0:T(8,128)(2,1)S(1)} %get-tuple-element.5, bf16[32,256,256]{2,1,0:T(8,128)(2,1)S(1)} %get-tuple-element.6, bf16[32,256,256]{2,1,0:T(8,128)(2,1)S(1)} %fusion.22), kind=kLoop, calls=%fused_computation.6 | loop fusion | flops 33554432 | bytes 29360128 | tf_op jit(solution)/shard_map/stack | solution.py:33
  147.1 58.1 %all-to-all-done = bf16[4,64,24,256]{3,1,2,0:T(8,128)(2,1)S(1)} async-done(((bf16[4,64,24,256]{3,1,2,0:T(8,128)(2,1)}), bf16[4,64,24,256]{3,1,2,0:T(8,128)(2,1)S(1)}, u32[]{:S(2)}, u32[]{:S(2)}) %all-to-all-start) | async-done | bytes 3145760 | tf_op jit(solution)/shard_map/all_to_all | solution.py:59
  205.1 1.8 copy.39
  206.9 7.5 %bitcast_convert_fusion.1 = bf16[32,96,512]{2,1,0:T(8,128)(2,1)S(1)} fusion(bf16[32,2,96,256]{3,2,1,0:T(8,128)(2,1)S(1)} %bitcast.51, bf16[32,1,256,512]{3,2,1,0:T(8,128)(2,1)} %get-tuple-element.8, bf16[32,1,256,512]{3,2,1,0:T(8,128)(2,1)} %get-tuple-element.7), kind=kOutput, calls=%fused_computation.9 | convolution fusion | flops 1620574208 | bytes 23068672 | tf_op jit(solution)/shard_map/mplc,mpcd->mld/dot_general | solution.py:36
  214.4 0.2 copy.43
  214.7 73.6 %all_to_all.10 = bf16[4,32,24,512]{3,2,1,0:T(8,128)(2,1)} all-to-all(bf16[4,32,24,512]{3,2,1,0:T(8,128)(2,1)S(1)} %bitcast.49), channel_id=1, replica_groups=mesh['grp'=2,'lon'=4,'lat'=4] {'lat'}, dimensions={0} | all-to-all | bytes 6291456 | tf_op jit(solution)/shard_map/all_to_all | solution.py:69
  288.2 0.0 all-gather.2.cloned.1.call-update
  288.3 6.9 %multiply_convert_fusion.1 = (bf16[512,1,720]{0,2,1:T(8,128)(2,1)S(1)}, bf16[512,1,720]{0,2,1:T(8,128)(2,1)S(1)}) fusion(f32[512]{0:T(512)S(1)} %select_multiply_fusion, s32[720]{0:T(1024)S(1)} %iota_add_fusion), kind=kLoop, calls=%fused_computation.20 | loop fusion | flops 5160960 | bytes 1479488 | tf_op jit(solution)/shard_map/convert.2
  295.2 73.4 %all-gather.2.cloned.1.call-done = bf16[512,24,512]{2,1,0:T(8,128)(2,1)} async-done(((bf16[128,24,512]{2,1,0:T(8,128)(2,1)}), bf16[512,24,512]{2,1,0:T(8,128)(2,1)}) %all-gather.2.cloned.1.call-update) | async-done | bytes 12582928 | tf_op jit(solution)/shard_map/all_gather | solution.py:75
  368.7 17.1 %copy.32 = bf16[512,24,512]{0,2,1:T(8,128)(2,1)} copy(bf16[512,24,512]{2,1,0:T(8,128)(2,1)} %all-gather.2.cloned.1.call-done) | data formatting | bytes 25165824 | tf_op jit(solution)/shard_map/all_gather | solution.py:75
  385.8 16.5 %fusion.4 = bf16[24,720,256]{2,1,0:T(8,128)(2,1)} fusion(bf16[512,24,2,256]{0,3,2,1:T(8,128)(2,1)} %bitcast.47, bf16[512,1,720]{0,2,1:T(8,128)(2,1)S(1)} %get-tuple-element.10, bf16[512,1,720]{0,2,1:T(8,128)(2,1)S(1)} %get-tuple-element.9), kind=kOutput, calls=%fused_computation.5 | convolution fusion | flops 9067069440 | bytes 22904832 | tf_op jit(solution)/shard_map/mlpc,mpn->lnc/dot_general | solution.py:79
  (3 shorter events, 0.0 us)
Async XLA Ops:
  6.5 119.3 %reduce-scatter.2.cloned.1.call-start = ((), (), s32[]{:S(2)}) async-start(), calls=%async_computation.3 | async-start | bytes 15728640 | tf_op jit(solution)/shard_map/reduce_scatter | solution.py:49
  129.8 75.3 %all-to-all-start = ((bf16[4,64,24,256]{3,1,2,0:T(8,128)(2,1)}), bf16[4,64,24,256]{3,1,2,0:T(8,128)(2,1)S(1)}, u32[]{:S(2)}, u32[]{:S(2)}) async-start(bf16[4,64,24,256]{3,1,2,0:T(8,128)(2,1)} %copy.26), calls=%async_computation.1 | async-start | bytes 6291456 | tf_op jit(solution)/shard_map/all_to_all | solution.py:59
  134.5 234.2 %all-gather.2.cloned.1.call-start = ((), (), s32[]{:S(2)}) async-start(), calls=%async_computation.4 | async-start | bytes 15728640 | tf_op jit(solution)/shard_map/all_gather | solution.py:75
Sparse Core Ops, SparseCore 0:
  24.0 101.7 reduce-scatter.1
  288.4 80.2 all-gather.1
where the time goes:
time: 410 us; the launch traced here: 409 us
  waiting for transfers between devices  233 us (57%)
  blocking collectives  73.6 us (18%)
  matrix products  35.9 us (9%)
  local copies, waits for them, and re-layouts  28.9 us (7%)
  other arithmetic  19.3 us (5%)
  between operations  13.5 us (3%)
  starting transfers between devices  4.61 us (1%)
    reduce_scatter x1, waiting for transfers between devices, on_device(): lax.psum_scatter(jnp.einsum('kn,lnc->klc', table_rows, grid_field, prefer...  102 us
    all_to_all x1, blocking collectives, on_device(): lax.all_to_all(back, 'lat', 0, 0, tiled=True)  73.6 us
    all_gather x1, waiting for transfers between devices, on_device(): portion = lax.all_gather(mixed_spec, 'lon', axis=0, tiled=True)  73.4 us
    all_to_all x1, waiting for transfers between devices, on_device(): lax.all_to_all(summed.reshape(lat_count, 2 * own_modes, lat_rows, channel...  58.1 us
    all_gather x1, local copies, waits for them, and re-layouts, on_device(): portion = lax.all_gather(mixed_spec, 'lon', axis=0, tiled=True)  17.1 us
    dot_general x1, matrix products, on_device(): jnp.einsum('mlpc,mpn->lnc', parted, table_rows, preferred_element_type=jn...  16.5 us
    dot_general x1, matrix products, on_device(): jnp.einsum('kn,lnc->klc', table_rows, grid_field, preferred_element_type=...  11.8 us
    another operation x2, other arithmetic  10.5 us
  transfers between devices with their start and end apart: 3, of which 3 were waited for; matrix products, arithmetic and copies ran while one was open for 5% of the time, Pallas kernels for 0%

commit v1 on v0

--- a/solution.py
+++ b/solution.py
@@ -3,6 +3,7 @@
 import jax.numpy as jnp
 from jax import lax
 from jax.sharding import PartitionSpec as P
+from jax.lax import axis_index, ppermute, psum
 
 NLON = 1440
 M = 512
@@ -72,7 +73,26 @@
     out_dev = 2 * NLON // lon_count
     out_index = lon_rank * out_dev + jnp.arange(out_dev, dtype=jnp.int32)
     inv_local = synthesis_table(out_index).reshape(M, 2, out_dev)
-    portion = lax.all_gather(mixed_spec, "lon", axis=0, tiled=True)
+    left_arr = psum(1, axis_name="lon")
+    field_out, mat_out, taken_in = (left_arr, axis_index("lon"), mixed_spec.shape[0])
+    by_place = [(nth, (nth + 1) % field_out) for nth in range(field_out)]
+    gallery = [(nth, (nth - 1) % field_out) for nth in range(field_out)]
+    portion = jnp.zeros(
+        (*mixed_spec.shape[:0], field_out * taken_in, *mixed_spec.shape[1:]), mixed_spec.dtype
+    )
+    portion = lax.dynamic_update_slice_in_dim(portion, mixed_spec, mat_out * taken_in, axis=0)
+    reply = raw_out = mixed_spec
+    carry_out = field_out // 2
+    for k0 in range(1, carry_out + 1):
+        reply = ppermute(reply, axis_name="lon", perm=by_place)
+        portion = lax.dynamic_update_slice_in_dim(
+            portion, reply, (mat_out - k0) % field_out * taken_in, axis=0
+        )
+        if k0 < field_out - carry_out:
+            raw_out = ppermute(raw_out, "lon", perm=gallery)
+            portion = lax.dynamic_update_slice_in_dim(
+                portion, raw_out, (mat_out + k0) % field_out * taken_in, axis=0
+            )
     count = portion.shape[0]
     table_rows = inv_local
     parted = portion.reshape(count, lat_rows, 2, channels)

time: 410 us -> 424 us (1.034)
  local copies, waits for them, and re-layouts: 28.9 us -> 44.2 us
    all_gather x1 -> x0, waiting for transfers between devices: 73.4 us -> none  [on_device(): portion = lax.all_gather(mixed_spec, 'lon', axis=0, tiled=True)]
    ppermute x0 -> x3, waiting for transfers between devices: none -> 70.3 us  [the longest x2 70.2 us: on_device(): reply = ppermute(reply, axis_name='lon', perm=by_place)]
    all_gather x1 -> x0, local copies, waits for them, and re-layouts: 17.1 us -> none  [on_device(): portion = lax.all_gather(mixed_spec, 'lon', axis=0, tiled=True)]
    ppermute x0 -> x3, local copies, waits for them, and re-layouts: none -> 13.9 us  [the longest x2 8.68 us: on_device(): reply = ppermute(reply, axis_name='lon', perm=by_place)]
    dynamic_update_slice x0 -> x4, local copies, waits for them, and re-layouts: none -> 8.2 us  [the longest x2 3.92 us: on_device(): lax.dynamic_update_slice_in_dim(portion, reply, (mat_out - k0) % field_ou...]
    broadcast_in_dim x0 -> x1, local copies, waits for them, and re-layouts: none -> 5.88 us  [on_device(): jnp.zeros((*mixed_spec.shape[:0], field_out * taken_in, *mixed_spec.shape...]
  transfers between devices with their start and end apart: 3 -> 5, of which waited for: 3 -> 4; matrix products, arithmetic and copies ran while one was open for 5% -> 11% of each run, Pallas kernels for 0% -> 0%
where the time goes in v1:
time: 424 us
  waiting for transfers between devices  230 us (54%)
  blocking collectives  72.7 us (17%)
  local copies, waits for them, and re-layouts  44.2 us (10%)
  matrix products  36.2 us (9%)
  other arithmetic  20.3 us (5%)
  between operations  13.5 us (3%)
  starting transfers between devices  6.36 us (2%)
    reduce_scatter x1, waiting for transfers between devices, on_device(): lax.psum_scatter(jnp.einsum('kn,lnc->klc', table_rows, grid_field, prefer...  102 us
    all_to_all x1, blocking collectives, on_device(): lax.all_to_all(back, 'lat', 0, 0, tiled=True)  72.7 us
    ppermute x2, waiting for transfers between devices, on_device(): reply = ppermute(reply, axis_name='lon', perm=by_place)  70.2 us
    all_to_all x1, waiting for transfers between devices, on_device(): lax.all_to_all(summed.reshape(lat_count, 2 * own_modes, lat_rows, channel...  58.1 us
    dot_general x1, matrix products, on_device(): jnp.einsum('mlpc,mpn->lnc', parted, table_rows, preferred_element_type=jn...  16.9 us
    dot_general x1, matrix products, on_device(): jnp.einsum('kn,lnc->klc', table_rows, grid_field, preferred_element_type=...  11.8 us
    another operation x2, other arithmetic  11.5 us
    ppermute x2, local copies, waits for them, and re-layouts, on_device(): reply = ppermute(reply, axis_name='lon', perm=by_place)  8.68 us
  transfers between devices with their start and end apart: 5, of which 4 were waited for; matrix products, arithmetic and copies ran while one was open for 11% of the time, Pallas kernels for 0%

profile of v1, /device:TPU:0, one launch (start us, length us, event | category | flops | bytes accessed | tf_op | source)
XLA Modules:
  0.0 423.6 jit_solution(7855769295351368817)
XLA Ops:
  6.5 3.6 multiply_convert_fusion.3
  12.1 11.8 %convolution_convert_fusion = bf16[1024,24,256]{2,0,1:T(8,128)(2,1)} fusion(bf16[24,360,256]{2,1,0:T(8,128)(2,1)} %param.2, bf16[1024,360]{1,0:T(8,128)(2,1)S(1)} %convert_element_type.48), kind=kOutput, calls=%fused_computation.8 | convolution fusion | flops 4536139776 | bytes 17743872 | tf_op jit(solution)/shard_map/kn,lnc->klc/dot_general | solution.py:51
  23.9 101.9 %reduce-scatter.2.cloned.1.call-done = bf16[256,24,256]{2,0,1:T(8,128)(2,1)} async-done(((bf16[1024,24,256]{2,0,1:T(8,128)(2,1)}), bf16[256,24,256]{2,0,1:T(8,128)(2,1)}) %reduce-scatter.2.cloned.1.call-update) | async-done | bytes 3145744 | tf_op jit(solution)/shard_map/reduce_scatter | solution.py:50
  125.8 4.0 copy.32
  129.9 4.6 %all-to-all-start = ((bf16[4,64,24,256]{3,1,2,0:T(8,128)(2,1)}), bf16[4,64,24,256]{3,1,2,0:T(8,128)(2,1)S(1)}, u32[]{:S(2)}, u32[]{:S(2)}) async-start(bf16[4,64,24,256]{3,1,2,0:T(8,128)(2,1)} %copy.32), calls=%async_computation.1 | async-start | bytes 6291456 | tf_op jit(solution)/shard_map/all_to_all | solution.py:60
  134.5 2.5 fusion.22
  136.9 3.8 slice_bitcast_fusion
  140.8 6.3 %maximum_bitcast_fusion = (bf16[32,1,256,512]{3,2,1,0:T(8,128)(2,1)}, bf16[32,1,256,512]{3,2,1,0:T(8,128)(2,1)}) fusion(bf16[32,256,256]{2,1,0:T(8,128)(2,1)S(1)} %get-tuple-element.5, bf16[32,256,256]{2,1,0:T(8,128)(2,1)S(1)} %get-tuple-element.6, bf16[32,256,256]{2,1,0:T(8,128)(2,1)S(1)} %fusion.22), kind=kLoop, calls=%fused_computation.6 | loop fusion | flops 33554432 | bytes 29360128 | tf_op jit(solution)/shard_map/stack | solution.py:34
  147.1 58.1 %all-to-all-done = bf16[4,64,24,256]{3,1,2,0:T(8,128)(2,1)S(1)} async-done(((bf16[4,64,24,256]{3,1,2,0:T(8,128)(2,1)}), bf16[4,64,24,256]{3,1,2,0:T(8,128)(2,1)S(1)}, u32[]{:S(2)}, u32[]{:S(2)}) %all-to-all-start) | async-done | bytes 3145760 | tf_op jit(solution)/shard_map/all_to_all | solution.py:60
  206.9 7.5 %bitcast_convert_fusion.1 = bf16[32,96,512]{2,1,0:T(8,128)(2,1)S(1)} fusion(bf16[32,2,96,256]{3,2,1,0:T(8,128)(2,1)S(1)} %bitcast.53, bf16[32,1,256,512]{3,2,1,0:T(8,128)(2,1)} %get-tuple-element.8, bf16[32,1,256,512]{3,2,1,0:T(8,128)(2,1)} %get-tuple-element.7), kind=kOutput, calls=%fused_computation.9 | convolution fusion | flops 1620574208 | bytes 23068672 | tf_op jit(solution)/shard_map/mplc,mpcd->mld/dot_general | solution.py:37
  214.7 72.7 %all_to_all.10 = bf16[4,32,24,512]{3,2,1,0:T(8,128)(2,1)S(1)} all-to-all(bf16[4,32,24,512]{3,2,1,0:T(8,128)(2,1)S(1)} %bitcast.51), channel_id=1, replica_groups=mesh['grp'=2,'lon'=4,'lat'=4] {'lat'}, dimensions={0} | all-to-all | bytes 6291456 | tf_op jit(solution)/shard_map/all_to_all | solution.py:70
  289.2 67.9 %collective-permute-done = bf16[128,24,512]{2,1,0:T(8,128)(2,1)} collective-permute-done((bf16[128,24,512]{2,1,0:T(8,128)(2,1)S(1)}, bf16[128,24,512]{2,1,0:T(8,128)(2,1)}, u32[]{:S(2)}, u32[]{:S(2)}) %collective-permute-start) | collective-permute-done | bytes 3145760 | tf_op jit(solution)/shard_map/ppermute | solution.py:87
  357.1 7.9 %multiply_convert_fusion.1 = (bf16[512,1,720]{0,2,1:T(8,128)(2,1)}, bf16[512,1,720]{0,2,1:T(8,128)(2,1)}) fusion(f32[512]{0:T(512)S(1)} %select_multiply_fusion, s32[720]{0:T(1024)S(1)} %iota_add_fusion), kind=kLoop, calls=%fused_computation.20 | loop fusion | flops 5160960 | bytes 1479488 | tf_op jit(solution)/shard_map/convert.2
  365.0 3.4 copy.38
  368.4 5.9 %broadcast_in_dim.18 = bf16[512,24,512]{0,2,1:T(8,128)(2,1)} broadcast(bf16[]{:T(256)} %constant.67.clone.1), dimensions={} | broadcast | bytes 12582914 | tf_op jit(solution)/shard_map/broadcast_in_dim | solution.py:80
  374.3 2.1 constant_dynamic-update-slice_fusion.3
  376.4 4.9 %copy.39 = bf16[128,24,512]{0,2,1:T(8,128)(2,1)} copy(bf16[128,24,512]{2,1,0:T(8,128)(2,1)} %collective-permute-done) | data formatting | bytes 6291456 | tf_op jit(solution)/shard_map/ppermute | solution.py:87
  381.4 5.2 %copy.40 = bf16[128,24,512]{0,2,1:T(8,128)(2,1)} copy(bf16[128,24,512]{2,1,0:T(8,128)(2,1)} %collective-permute-done.1) | data formatting | bytes 6291456 | tf_op jit(solution)/shard_map/ppermute | solution.py:92
  386.6 1.9 constant_dynamic-update-slice_fusion.2
  389.6 2.2 constant_dynamic-update-slice_fusion.1
  391.8 2.3 collective-permute-done.2
  394.1 3.8 copy.41
  397.9 2.0 constant_dynamic-update-slice_fusion
  399.9 16.9 %fusion.4 = bf16[24,720,256]{2,1,0:T(8,128)(2,1)} fusion(bf16[512,24,2,256]{0,3,2,1:T(8,128)(2,1)} %bitcast.47, bf16[512,1,720]{0,2,1:T(8,128)(2,1)S(1)} %copy-done.4, bf16[512,1,720]{0,2,1:T(8,128)(2,1)S(1)} %copy-done.3), kind=kOutput, calls=%fused_computation.5 | convolution fusion | flops 9067069440 | bytes 22904832 | tf_op jit(solution)/shard_map/mlpc,mpn->lnc/dot_general | solution.py:99
  (24 shorter events, 6.8 us)
Async XLA Ops:
  6.5 119.3 %reduce-scatter.2.cloned.1.call-start = ((), (), s32[]{:S(2)}) async-start(), calls=%async_computation.3 | async-start | bytes 15728640 | tf_op jit(solution)/shard_map/reduce_scatter | solution.py:50
  129.9 75.3 %all-to-all-start = ((bf16[4,64,24,256]{3,1,2,0:T(8,128)(2,1)}), bf16[4,64,24,256]{3,1,2,0:T(8,128)(2,1)S(1)}, u32[]{:S(2)}, u32[]{:S(2)}) async-start(bf16[4,64,24,256]{3,1,2,0:T(8,128)(2,1)} %copy.32), calls=%async_computation.1 | async-start | bytes 6291456 | tf_op jit(solution)/shard_map/all_to_all | solution.py:60
  287.4 69.7 %collective-permute-start = (bf16[128,24,512]{2,1,0:T(8,128)(2,1)S(1)}, bf16[128,24,512]{2,1,0:T(8,128)(2,1)}, u32[]{:S(2)}, u32[]{:S(2)}) collective-permute-start(bf16[128,24,512]{2,1,0:T(8,128)(2,1)S(1)} %bitcast.48), channel_id=1, source_target_pairs={{0,4},{4,8},{8,12},{12,0},{1,5},{5,9},{9,13},{13,1},{2,6},{6,10},{... | collective-permute-start | bytes 9437192 | tf_op jit(solution)/shard_map/ppermute | solution.py:87
  287.4 93.9 %collective-permute-start.1 = (bf16[128,24,512]{2,1,0:T(8,128)(2,1)S(1)}, bf16[128,24,512]{2,1,0:T(8,128)(2,1)}, u32[]{:S(2)}, u32[]{:S(2)}) collective-permute-start(bf16[128,24,512]{2,1,0:T(8,128)(2,1)S(1)} %bitcast.49), channel_id=1, source_target_pairs={{0,12},{4,0},{8,4},{12,8},{1,13},{5,1},{9,5},{13,9},{2,14},{6,2},{... | collective-permute-start | bytes 9437192 | tf_op jit(solution)/shard_map/ppermute | solution.py:92
  357.1 37.0 %collective-permute-start.2 = (bf16[128,24,512]{2,1,0:T(8,128)(2,1)}, bf16[128,24,512]{2,1,0:T(8,128)(2,1)}, u32[]{:S(2)}, u32[]{:S(2)}) collective-permute-start(bf16[128,24,512]{2,1,0:T(8,128)(2,1)} %collective-permute-done), channel_id=1, source_target_pairs={{0,4},{4,8},{8,12},{12,0},{1,5},{5,9},{9,13},{13,1},{2,6},{6,10},{... | collective-permute-start | bytes 9437192 | tf_op jit(solution)/shard_map/ppermute | solution.py:87
  368.4 5.9 %copy-start.2 = (bf16[128,24,512]{0,2,1:T(8,128)(2,1)S(1)}, bf16[128,24,512]{0,2,1:T(8,128)(2,1)}, u32[]{:S(2)}) copy-start(bf16[128,24,512]{0,2,1:T(8,128)(2,1)} %copy.38) | copy-start | bytes 9437188
  381.4 5.2 %copy-start = (bf16[128,24,512]{0,2,1:T(8,128)(2,1)S(1)}, bf16[128,24,512]{0,2,1:T(8,128)(2,1)}, u32[]{:S(2)}) copy-start(bf16[128,24,512]{0,2,1:T(8,128)(2,1)} %copy.39) | copy-start | bytes 9437188
  386.6 3.0 copy-start.1
  397.9 2.0 copy-start.3
  397.9 2.0 copy-start.4
Sparse Core Ops, SparseCore 0:
  24.1 101.7 reduce-scatter.1
